TPU v7x, 128 devices: a whole 4x4x4 slice. The times are simulated.
128 devices in a mesh: dp: 32 (over z, x, core), col: 4 (over y).
Axes of the slice: x: 4, y: 4, z: 4, core: 2. Of those that a mesh axis runs over, the one named last changes fastest.
Arguments:
- activations: bfloat16 [16384, 16384], P('dp', 'col'), may hold values from -18 to 18
- out_grads: bfloat16 [16384, 53248], P('dp', 'col'), may hold values from -18 to 18
- sketch: bfloat16 [53248, 128], P('col'), may hold values from -6 to 6
Outputs:
- adapter_b: float32 [16384, 64], P(('col', 'dp'))
- adapter_a_t: float32 [53248, 64], P(('col', 'dp'))
All inputs are finite; a program needn't handle non-finite values.
Results may differ from a plain program's by a relative error of at most 0.005.
Values may be sent and summed in bfloat16 or wider, within the bound.
A program may use at most 128 MiB of HBM per device.

v0:
```python
import jax
import jax.numpy as jnp
from jax import lax
from jax.sharding import PartitionSpec as P

D = 16384
F = 53248
RANK = 64
ITERS = 2


def copy_for_each(x, axis):
    count = lax.axis_size(axis)
    return lax.all_to_all(jnp.broadcast_to(x[None], (count, *x.shape)), axis, 0, 0, tiled=True)


def over_copies(x, axis):
    everything = copy_for_each(x, axis)
    return jnp.sum(everything, axis=0)


def cut_along(x, dim, count):
    lengths = x.shape
    pieces = x.reshape(*lengths[:dim], count, lengths[dim] // count, *lengths[dim + 1 :])
    return jnp.moveaxis(pieces, dim, 0)


def sum_at_owner(x, axis, dim):
    count = lax.axis_size(axis)
    pieces = lax.all_to_all(cut_along(x, dim, count), axis, 0, 0, tiled=True)
    return jnp.sum(pieces, axis=0)


def total_of_pieces(x, axis):
    return lax.all_gather(x, axis).sum(0)


def laid_out(pieces, dim):
    pieces = jnp.moveaxis(pieces, 0, dim)
    lengths = pieces.shape
    return pieces.reshape(*lengths[:dim], lengths[dim] * lengths[dim + 1], *lengths[dim + 2 :])


def gather_directly(x, axis, dim):
    pieces = copy_for_each(x, axis)
    return laid_out(pieces, dim)


def cholesky_basis(panel_in, gram_matrix, row_total):
    width = panel_in.shape[1]
    identity_k = jnp.eye(width, dtype=jnp.float32)
    shift_value = 1e-05 * jnp.trace(gram_matrix) / width
    lower_factor = jnp.linalg.cholesky(gram_matrix + shift_value * identity_k)
    inverse = jax.scipy.linalg.solve_triangular(lower_factor, identity_k, lower=True)
    scaled = jnp.dot(
        panel_in, inverse.T, precision=lax.Precision.HIGHEST, preferred_element_type=jnp.float32
    )
    return scaled * jnp.float32(row_total**0.5)


def local_gram(panel_in):
    return jnp.dot(
        panel_in.T, panel_in, precision=lax.Precision.HIGHEST, preferred_element_type=jnp.float32
    )


def body(activations, out_grads, sketch):
    dp_count = lax.axis_size("dp")
    hidden_local = out_grads.shape[1]
    hidden_rows = hidden_local // dp_count
    right_b = sketch
    left_rows_q = None
    right_rows_p = None
    for iteration in range(ITERS):
        left_part = jnp.dot(out_grads, right_b, preferred_element_type=jnp.float32)
        left_s = over_copies(left_part, "col").astype(jnp.bfloat16)
        left_y = sum_at_owner(
            lax.dot_general(
                activations, left_s, (((0,), (0,)), ((), ())), preferred_element_type=jnp.float32
            ),
            "dp",
            0,
        )
        gram_left = total_of_pieces(local_gram(left_y), ("dp", "col"))
        left_rows_q = cholesky_basis(left_y, gram_left, D)
        left_b = left_rows_q.astype(jnp.bfloat16)
        right_part = jnp.dot(
            activations, gather_directly(left_b, "dp", 0), preferred_element_type=jnp.float32
        )
        right_t = over_copies(right_part, "col").astype(jnp.bfloat16)
        whole_part = lax.dot_general(
            out_grads, right_t, (((0,), (0,)), ((), ())), preferred_element_type=jnp.float32
        )
        right_full = lax.psum(whole_part, "dp")
        gram_right = over_copies(local_gram(right_full), "col")
        right_whole_p = cholesky_basis(right_full, gram_right, F)
        right_b = right_whole_p.astype(jnp.bfloat16)
        right_rows_p = lax.dynamic_slice_in_dim(
            right_whole_p, lax.axis_index("dp") * hidden_rows, hidden_rows, 0
        )
    return (left_rows_q[:, :RANK], right_rows_p[:, RANK:])


def solution(mesh):
    return jax.shard_map(
        body,
        mesh=mesh,
        in_specs=(P("dp", "col"), P("dp", "col"), P("col", None)),
        out_specs=(P(("col", "dp"), None), P(("col", "dp"), None)),
        check_vma=False,
    )
```

profile of v0, /device:TPU:1, one launch (start us, length us, event | category | flops | bytes accessed | tf_op | source)
XLA Modules:
  0.0 802.3 jit_solution(13290955720750246626)
XLA Ops:
  7.2 1.9 copy-done
  9.1 7.1 fusion.27
  16.3 19.0 %all_to_all.50 = f32[4,512,128]{2,1,0:T(8,128)S(1)} all-to-all(f32[4,512,128]{2,1,0:T(8,128)S(1)} %broadcast_in_dim.24), channel_id=1, replica_groups=mesh['dp'=32,'col'=4] {'col'}, dimensions={0} | all-to-all | bytes 2097152 | tf_op jit(solution)/shard_map/all_to_all | solution.py:14
  35.3 2.9 convolution_bitcast_fusion.3
  38.5 38.0 %all_to_all.51 = f32[32,128,128]{1,2,0:T(8,128)S(1)} all-to-all(f32[32,128,128]{1,2,0:T(8,128)S(1)} %bitcast.97), channel_id=1, replica_groups=mesh['dp'=32,'col'=4] {'dp'}, dimensions={0} | all-to-all | bytes 4194304 | tf_op jit(solution)/shard_map/all_to_all | solution.py:30
  76.6 0.9 fusion.28
  77.6 66.2 %all-gather.5.cloned.1.call-done = f32[16384,128]{1,0:T(8,128)} async-done(((f32[128,128]{1,0:T(8,128)}), f32[16384,128]{1,0:T(8,128)}) %all-gather.5.cloned.1.call-update) | async-done | bytes 8388624 | tf_op jit(solution)/shard_map/all_gather | solution.py:35
  143.8 3.8 reduce_sum.120
  149.1 11.7 %cholesky.74 = f32[128,128]{1,0:T(8,128)S(1)} custom-call(f32[128,128]{1,0:T(8,128)S(1)} %fusion.25), custom_call_target="Cholesky" | custom-call | tf_op jit(solution)/shard_map/jit(cholesky)/cholesky | solution.py:53
  161.5 0.7 fusion.14
  162.2 9.8 %custom-call.8 = f32[1,128,128]{1,2,0:T(8,128)S(1)} custom-call(f32[1,128,128]{2,1,0:T(8,128)S(1)} %fusion.14), custom_call_target="InvertDiagBlocksLowerTriangular" | custom-call | tf_op jit(solution)/shard_map/jit(_solve_triangular)/triangular_solve | solution.py:54
  172.8 21.9 %all_to_all.52 = bf16[32,128,128]{2,1,0:T(8,128)(2,1)S(1)} all-to-all(bf16[32,128,128]{2,1,0:T(8,128)(2,1)S(1)} %broadcast_in_dim.26), channel_id=1, replica_groups=mesh['dp'=32,'col'=4] {'dp'}, dimensions={0} | all-to-all | bytes 2097152 | tf_op jit(solution)/shard_map/all_to_all | solution.py:14
  194.7 3.7 convolution_bitcast_fusion.5
  198.7 16.8 %all_to_all.53 = f32[4,512,128]{2,1,0:T(8,128)S(1)} all-to-all(f32[4,512,128]{2,1,0:T(8,128)S(1)} %broadcast_in_dim.27), channel_id=1, replica_groups=mesh['dp'=32,'col'=4] {'col'}, dimensions={0} | all-to-all | bytes 2097152 | tf_op jit(solution)/shard_map/all_to_all | solution.py:14
  215.5 9.8 %convolution_bitcast_fusion.1 = f32[13312,128]{0,1:T(8,128)} fusion(bf16[512,13312]{1,0:T(8,128)(2,1)} %param.7, bf16[512,128]{1,0:T(8,128)(2,1)S(1)} %reduce_sum.122), kind=kOutput, calls=%fused_computation.2 | convolution fusion | flops 1744830464 | bytes 20578304 | tf_op jit(solution)/shard_map/dot_general | solution.py:91
  225.4 114.0 %all-reduce.3.cloned.1.call-done = f32[13312,128]{0,1:T(8,128)} async-done(((f32[13312,128]{0,1:T(8,128)}), f32[13312,128]{0,1:T(8,128)}) %all-reduce.3.cloned.1.call-update) | async-done | bytes 6815760 | tf_op jit(solution)/shard_map/psum | solution.py:94
  339.3 8.8 %fusion.29 = f32[128,128]{1,0:T(8,128)S(1)} fusion(f32[13312,128]{0,1:T(8,128)} %all-reduce.3.cloned.1.call-done), kind=kOutput, calls=%fused_computation.69 | convolution fusion | flops 2617245696 | bytes 6881280 | tf_op jit(solution)/shard_map/dot_general | solution.py:62
  348.1 9.4 %all_to_all.54 = f32[4,128,128]{2,1,0:T(8,128)S(1)} all-to-all(f32[4,128,128]{2,1,0:T(8,128)S(1)} %broadcast_in_dim.28), channel_id=1, replica_groups=mesh['dp'=32,'col'=4] {'col'}, dimensions={0} | all-to-all | bytes 524288 | tf_op jit(solution)/shard_map/all_to_all | solution.py:14
  359.0 11.7 %cholesky.85 = f32[128,128]{1,0:T(8,128)S(1)} custom-call(f32[128,128]{1,0:T(8,128)S(1)} %fusion.23), custom_call_target="Cholesky" | custom-call | tf_op jit(solution)/shard_map/jit(cholesky)/cholesky | solution.py:53
  371.4 0.7 fusion.15
  372.1 9.8 %custom-call.9 = f32[1,128,128]{1,2,0:T(8,128)S(1)} custom-call(f32[1,128,128]{2,1,0:T(8,128)S(1)} %fusion.15), custom_call_target="InvertDiagBlocksLowerTriangular" | custom-call | tf_op jit(solution)/shard_map/jit(_solve_triangular)/triangular_solve | solution.py:54
  382.2 22.8 %fusion = bf16[13312,128]{1,0:T(8,128)(2,1)S(1)} fusion(f32[13312,128]{0,1:T(8,128)} %all-reduce.3.cloned.1.call-done, f32[128,128]{1,0:T(8,128)S(1)} %fusion.6), kind=kOutput, calls=%fused_computation.3 | convolution fusion | flops 2620653568 | bytes 10289152 | tf_op jit(solution)/shard_map/dot_general | solution.py:55
  405.0 10.2 %convolution_bitcast_fusion.6 = f32[512,128]{0,1:T(8,128)} fusion(bf16[13312,128]{1,0:T(8,128)(2,1)S(1)} %fusion, bf16[512,13312]{1,0:T(8,128)(2,1)} %param.7), kind=kOutput, calls=%fused_computation.10 | convolution fusion | flops 1744830464 | bytes 17301504 | tf_op jit(solution)/shard_map/dot_general | solution.py:75
  415.2 1.1 copy.42
  416.3 15.1 %all_to_all.55 = f32[4,512,128]{2,1,0:T(8,128)S(1)} all-to-all(f32[4,512,128]{2,1,0:T(8,128)S(1)} %broadcast_in_dim.29), channel_id=1, replica_groups=mesh['dp'=32,'col'=4] {'col'}, dimensions={0} | all-to-all | bytes 2097152 | tf_op jit(solution)/shard_map/all_to_all | solution.py:14
  431.5 2.9 convolution_bitcast_fusion.2
  434.7 38.4 %all_to_all.56 = f32[32,128,128]{1,2,0:T(8,128)S(1)} all-to-all(f32[32,128,128]{1,2,0:T(8,128)S(1)} %bitcast.98), channel_id=1, replica_groups=mesh['dp'=32,'col'=4] {'dp'}, dimensions={0} | all-to-all | bytes 4194304 | tf_op jit(solution)/shard_map/all_to_all | solution.py:30
  473.2 0.9 fusion.30
  474.2 66.2 %all-gather.7.cloned.1.call-done = f32[16384,128]{1,0:T(8,128)} async-done(((f32[128,128]{1,0:T(8,128)}), f32[16384,128]{1,0:T(8,128)}) %all-gather.7.cloned.1.call-update) | async-done | bytes 8388624 | tf_op jit(solution)/shard_map/all_gather | solution.py:35
  540.4 3.8 reduce_sum.127
  545.7 11.7 %cholesky.96 = f32[128,128]{1,0:T(8,128)S(1)} custom-call(f32[128,128]{1,0:T(8,128)S(1)} %fusion.21), custom_call_target="Cholesky" | custom-call | tf_op jit(solution)/shard_map/jit(cholesky)/cholesky | solution.py:53
  558.1 0.7 fusion.16
  558.8 9.8 %custom-call.10 = f32[1,128,128]{1,2,0:T(8,128)S(1)} custom-call(f32[1,128,128]{2,1,0:T(8,128)S(1)} %fusion.16), custom_call_target="InvertDiagBlocksLowerTriangular" | custom-call | tf_op jit(solution)/shard_map/jit(_solve_triangular)/triangular_solve | solution.py:54
  569.4 21.6 %all_to_all.57 = bf16[32,128,128]{2,1,0:T(8,128)(2,1)S(1)} all-to-all(bf16[32,128,128]{2,1,0:T(8,128)(2,1)S(1)} %broadcast_in_dim.30), channel_id=1, replica_groups=mesh['dp'=32,'col'=4] {'dp'}, dimensions={0} | all-to-all | bytes 2097152 | tf_op jit(solution)/shard_map/all_to_all | solution.py:14
  591.0 3.7 convolution_bitcast_fusion.4
  594.9 17.0 %all_to_all.58 = f32[4,512,128]{2,1,0:T(8,128)S(1)} all-to-all(f32[4,512,128]{2,1,0:T(8,128)S(1)} %broadcast_in_dim.31), channel_id=1, replica_groups=mesh['dp'=32,'col'=4] {'col'}, dimensions={0} | all-to-all | bytes 2097152 | tf_op jit(solution)/shard_map/all_to_all | solution.py:14
  612.0 9.8 %convolution_bitcast_fusion = f32[13312,128]{0,1:T(8,128)} fusion(bf16[512,13312]{1,0:T(8,128)(2,1)} %param.7, bf16[512,128]{1,0:T(8,128)(2,1)S(1)} %reduce_sum.129), kind=kOutput, calls=%fused_computation | convolution fusion | flops 1744830464 | bytes 20578304 | tf_op jit(solution)/shard_map/dot_general | solution.py:91
  621.8 114.2 %all-reduce.5.cloned.1.call-done = f32[13312,128]{0,1:T(8,128)} async-done(((f32[13312,128]{0,1:T(8,128)}), f32[13312,128]{0,1:T(8,128)}) %all-reduce.5.cloned.1.call-update) | async-done | bytes 6815760 | tf_op jit(solution)/shard_map/psum | solution.py:94
  736.0 8.8 %fusion.31 = f32[128,128]{1,0:T(8,128)S(1)} fusion(f32[13312,128]{0,1:T(8,128)} %all-reduce.5.cloned.1.call-done), kind=kOutput, calls=%fused_computation.71 | convolution fusion | flops 2617245696 | bytes 6881280 | tf_op jit(solution)/shard_map/dot_general | solution.py:62
  744.8 0.7 broadcast_in_dim.32
  745.5 4.0 all-to-all-start.9
  749.5 0.7 copy.53
  750.2 4.9 all-to-all-done.9
  756.6 11.7 %cholesky.107 = f32[128,128]{1,0:T(8,128)S(1)} custom-call(f32[128,128]{1,0:T(8,128)S(1)} %fusion.19), custom_call_target="Cholesky" | custom-call | tf_op jit(solution)/shard_map/jit(cholesky)/cholesky | solution.py:53
  769.7 9.8 %custom-call.11 = f32[1,128,128]{1,2,0:T(8,128)S(1)} custom-call(f32[1,128,128]{2,1,0:T(8,128)S(1)} %fusion.17), custom_call_target="InvertDiagBlocksLowerTriangular" | custom-call | tf_op jit(solution)/shard_map/jit(_solve_triangular)/triangular_solve | solution.py:54
  779.8 13.1 %fusion.32 = f32[13312,128]{1,0:T(8,128)S(1)} fusion(f32[13312,128]{0,1:T(8,128)} %all-reduce.5.cloned.1.call-done, f32[128,128]{1,0:T(8,128)S(1)} %fusion.2), kind=kOutput, calls=%fused_computation.72 | convolution fusion | flops 2617245696 | bytes 13697024 | tf_op jit(solution)/shard_map/dot_general | solution.py:55
  792.9 0.8 dynamic-slice_multiply_fusion
  793.7 1.7 copy.54
  (65 shorter events, 10.6 us)
Async XLA Ops:
  7.2 2.0 copy-start
  7.2 136.6 %all-gather.5.cloned.1.call-start = ((), (), s32[]{:S(2)}) async-start(), calls=%async_computation.12 | async-start | bytes 8454144 | tf_op jit(solution)/shard_map/all_gather | solution.py:35
  77.6 261.8 %all-reduce.3.cloned.1.call-start = ((), (), s32[]{:S(2)}) async-start(), calls=%async_computation.10 | async-start | bytes 13631488 | tf_op jit(solution)/shard_map/psum | solution.py:94
  225.3 315.1 %all-gather.7.cloned.1.call-start = ((), (), s32[]{:S(2)}) async-start(), calls=%async_computation.13 | async-start | bytes 8454144 | tf_op jit(solution)/shard_map/all_gather | solution.py:35
  474.1 261.9 %all-reduce.5.cloned.1.call-start = ((), (), s32[]{:S(2)}) async-start(), calls=%async_computation.11 | async-start | bytes 13631488 | tf_op jit(solution)/shard_map/psum | solution.py:94
  745.5 9.6 %all-to-all-start.9 = ((f32[4,128,128]{2,1,0:T(8,128)}), f32[4,128,128]{2,1,0:T(8,128)S(1)}, u32[]{:S(2)}, u32[]{:S(2)}) async-start(f32[4,128,128]{2,1,0:T(8,128)} %broadcast_in_dim.32), calls=%async_computation.9 | async-start | bytes 524288 | tf_op jit(solution)/shard_map/all_to_all | solution.py:14
  779.5 15.9 %copy-start.1 = (bf16[13312,128]{1,0:T(8,128)(2,1)S(1)}, bf16[13312,128]{1,0:T(8,128)(2,1)}, u32[]{:S(2)}) copy-start(bf16[13312,128]{1,0:T(8,128)(2,1)} %param.8) | copy-start | bytes 10223620
Sparse Core Ops, SparseCore 0:
  77.7 66.1 all-gather.4
  225.4 113.8 all-reduce.2
  474.2 66.0 all-gather.6
  621.9 114.0 all-reduce.4
where the time goes:
time: 813 us; the launch traced here: 802 us
  waiting for transfers between devices  366 us (45%)
  blocking collectives  197 us (24%)
  matrix products  107 us (13%)
  other arithmetic  103 us (13%)
  between operations  17.2 us (2%)
  local copies, waits for them, and re-layouts  8.32 us (1%)
    psum x2, waiting for transfers between devices, body(): right_full = lax.psum(whole_part, 'dp')  228 us
    all_gather x2, waiting for transfers between devices, total_of_pieces(): return lax.all_gather(x, axis).sum(0)  132 us
    all_to_all x7, blocking collectives, copy_for_each(): lax.all_to_all(jnp.broadcast_to(x[None], (count, *x.shape)), axis, 0, 0,...  121 us
    all_to_all x2, blocking collectives, sum_at_owner(): pieces = lax.all_to_all(cut_along(x, dim, count), axis, 0, 0, tiled=True)  76.4 us
    another operation x12, other arithmetic, cholesky_basis(): lower_factor = jnp.linalg.cholesky(gram_matrix + shift_value * identity_k)  49.6 us
    another operation x8, other arithmetic, cholesky_basis(): jax.scipy.linalg.solve_triangular(lower_factor, identity_k, lower=True)  41.9 us
    dot_general x4, matrix products, cholesky_basis(): jnp.dot(panel_in, inverse.T, precision=lax.Precision.HIGHEST, preferred_e...  36.4 us
    dot_general x2, matrix products, body(): lax.dot_general(out_grads, right_t, (((0,), (0,)), ((), ())), preferred_e...  19.5 us
  transfers between devices with their start and end apart: 5, of which 5 were waited for; matrix products, arithmetic and copies ran while one was open for 0% of the time, Pallas kernels for 0%

commit v1 on v0

v1 whole, which is shorter than its diff:
```python
import functools

import jax
import jax.numpy as jnp
from jax import lax
from jax.experimental import pallas as pl
from jax.experimental.pallas import tpu as pltpu
from jax.sharding import PartitionSpec as P

RANK = 64
ITERS = 2
K = 128
f32 = jnp.float32
bf16 = jnp.bfloat16
HIGHEST = lax.Precision.HIGHEST
SIDE = 4


def lanes_of(x, k):
    return jnp.broadcast_to(x[:, k : k + 1], (8, K))


def row_of(x, k):
    return jnp.broadcast_to(x[k : k + 1, :], (8, K))


def inverse_factor(matrix):
    lane = lax.broadcasted_iota(jnp.int32, (8, K), 1)
    sub = lax.broadcasted_iota(jnp.int32, (8, K), 0)
    low = lane < 8
    eye = jnp.where(lane == sub, 1.0, 0.0).astype(f32)

    def block(limit):
        def step(b, rows):
            pivots = [lanes_of(rows[0], k) for k in range(8)]
            panel = jnp.where(low, eye, rows[0])
            recip, coef, done = [], {}, []
            scale = jnp.zeros((8, K), f32)
            for k in range(8):
                d = row_of(pivots[k], k)
                recip.append(1.0 / d)
                scale = jnp.where(sub == k, lax.rsqrt(d), scale)
                done.append(row_of(panel, k))
                if k < 7:
                    c = jnp.where(sub > k, pivots[k] * recip[k], 0.0)
                    for m in range(k + 1, 8):
                        coef[k, m] = row_of(pivots[m], k)
                        pivots[m] = pivots[m] - c * coef[k, m]
                    panel = panel - c * done[k]
            new = [panel * scale]
            for u in range(1, 16):
                if u >= limit:
                    new.append(rows[u])
                    continue
                cols = [lanes_of(rows[u], k) for k in range(8)]
                acc = jnp.where(low, 0.0, rows[u])
                for k in range(8):
                    ck = cols[k] * recip[k]
                    for m in range(k + 1, 8):
                        cols[m] = cols[m] - ck * coef[k, m]
                    acc = acc - ck * done[k]
                new.append(jnp.where(u < 16 - b, acc, rows[u]))
            new = [pltpu.roll(w, K - 8, 1) for w in new]
            return tuple(new[1:] + new[:1])

        return step

    rows = tuple(matrix[8 * u : 8 * u + 8, :] for u in range(16))
    for part in range(4):
        rows = lax.fori_loop(4 * part, 4 * part + 4, block(16 - 4 * part), rows)
    whole = jnp.concatenate(rows, axis=0)
    i = lax.broadcasted_iota(jnp.int32, (K, K), 0)
    j = lax.broadcasted_iota(jnp.int32, (K, K), 1)
    return jnp.where(j <= i, whole, 0.0)


def kernel(
    features, hidden, a_hbm, o_hbm, sk_hbm, q_ref, p_ref,
    a, o, sketch, load_sem,
    s_part, s_recv, s_mine, s_all, s_t, s_sem,
    gram_own, gram_first, gram_slots, gram_half, gram_all, gram_sem, factor_y, factor_z,
    *panel_refs,
):
    dp, y = lax.axis_index("dp"), lax.axis_index("col")
    z, x, c = dp // 8, lax.rem(dp // 2, SIDE), lax.rem(dp, 2)
    names = ("own", "c1s", "c1r", "a2s", "a2r", "b2s", "b2r", "a3s", "a3r", "b3s", "b3r", "shard", "gathered", "sem")
    half = len(names)
    bufs_y = dict(zip(names, panel_refs[:half]))
    bufs_z = dict(zip(names, panel_refs[half:]))

    def at(z_=None, x_=None, c_=None):
        z_ = z if z_ is None else z_
        x_ = x if x_ is None else x_
        c_ = c if c_ is None else c_
        return {"dp": (z_ * SIDE + x_) * 2 + c_, "col": y}

    def along(axis, j):
        if axis == "x":
            return at(x_=lax.rem(x + j, SIDE))
        if axis == "z":
            return at(z_=lax.rem(z + j, SIDE))
        if axis == "y":
            return {"dp": dp, "col": lax.rem(y + j, SIDE)}
        return at(c_=1 - c)

    pending = []

    def send(src, dst, sems, index, device):
        copy = pltpu.make_async_remote_copy(
            src_ref=src, dst_ref=dst, send_sem=sems.at[0, index], recv_sem=sems.at[1, index],
            device_id=device, device_id_type=pl.DeviceIdType.MESH,
        )
        copy.start()
        pending.append(copy)
        return copy

    def flush():
        for copy in pending:
            copy.wait_send()
        pending.clear()

    tokens = s_mine.shape[0]
    turn = [lax.rem(y + 1 + k, SIDE) for k in range(SIDE)]
    loads = [pltpu.make_async_copy(sk_hbm, sketch, load_sem.at[0])]
    for k in range(SIDE):
        span = pl.ds(pl.multiple_of(turn[k] * tokens, tokens), tokens)
        loads.append(pltpu.make_async_copy(o_hbm.at[span, :], o.at[span, :], load_sem.at[1 + k]))
    loads.append(pltpu.make_async_copy(a_hbm, a, load_sem.at[5]))
    for copy in loads:
        copy.start()

    barrier = pltpu.get_barrier_semaphore()
    partners = [along("core", 0)] + [along(axis, j) for axis in "xyz" for j in (1, 2, 3)]
    for device in partners:
        pl.semaphore_signal(barrier, inc=1, device_id=device, device_id_type=pl.DeviceIdType.MESH)
    pl.semaphore_wait(barrier, len(partners))

    def send_tokens(k):
        span = pl.ds(pl.multiple_of(turn[k] * tokens, tokens), tokens)
        return send(s_part.at[span, :], s_recv.at[k], s_sem, k, along("y", k + 1))

    def share_tokens(sends, factor):
        span = pl.ds(pl.multiple_of(y * tokens, tokens), tokens)
        total = s_part[span, :]
        for k in range(3):
            sends[k].wait_recv()
            total = total + s_recv[k]
        if factor is not None:
            total = lax.dot_general(
                total, factor(), (((1,), (1,)), ((), ())), precision=HIGHEST, preferred_element_type=f32
            )
        s_all[span, :] = total.astype(bf16)
        outs = [send(s_all.at[span, :], s_all.at[span, :], s_sem, 3 + k, along("y", k + 1)) for k in range(3)]
        for copy in outs:
            copy.wait_recv()
        flush()
        s_t[...] = s_all[...].T

    def reduce_panel(weights, bufs, columns):
        own, c1s, c1r, sem = bufs["own"], bufs["c1s"], bufs["c1r"], bufs["sem"]
        rows = own.shape[2]
        h = rows // 2
        zs = [lax.rem(z + 1 + k, SIDE) for k in range(SIDE)]
        span = columns // SIDE
        pieces = 1 if span % 1024 == 0 else 2
        first, second_a, second_b = [], [], []

        def compute(k):
            for piece in range(pieces):
                width = span // pieces
                n = SIDE // pieces
                start = pl.multiple_of(zs[k] * span + piece * width, K)
                r = jnp.dot(s_t[...], weights[:, pl.ds(start, width)], preferred_element_type=f32).T
                r = r.reshape(n, 2, rows, K)
                own[k, piece * n : (piece + 1) * n] = jnp.where(c == 0, r[:, 0], r[:, 1])
                c1s[k, piece * n : (piece + 1) * n] = jnp.where(c == 0, r[:, 1], r[:, 0]).astype(bf16)
            first.append(send(c1s.at[k], c1r.at[k], sem, k, along("core", 0)))

        def pass_on(k):
            first[k].wait_recv()
            for i in range(SIDE):
                v = own[k, i] + c1r[k, i].astype(f32)
                own[k, i] = v
                v = v.astype(bf16)
                bufs["a2s"][k, i] = v[:h]
                bufs["b2s"][k, i] = v[h:]
            for j in (1, 2, 3):
                there = lax.rem(x + j, SIDE)
                second_a.append(
                    send(bufs["a2s"].at[k, there], bufs["a2r"].at[k, j - 1], sem, 4 + k * 3 + j - 1, along("x", j))
                )
            if k < 3:
                second_b.append(send(bufs["b2s"].at[k], bufs["b2r"].at[k], sem, 16 + k, along("z", k + 1)))

        for k in range(SIDE):
            compute(k)
            if k > 0:
                pass_on(k - 1)
        pass_on(3)
        third_a, third_b = [], []
        for k in range(SIDE):
            total = own[k, x, :h, :]
            for j in range(3):
                second_a[k * 3 + j].wait_recv()
                total = total + bufs["a2r"][k, j].astype(f32)
            if k < 3:
                bufs["a3s"][k] = total.astype(bf16)
                third_a.append(send(bufs["a3s"].at[k], bufs["a3r"].at[k], sem, 19 + k, along("z", k + 1)))
            else:
                mine_a = total
        for k in range(3):
            second_b[k].wait_recv()
        for k in range(SIDE):
            there = lax.rem(x + 1 + k, SIDE)
            total = own[3, there, h:, :]
            for j in range(3):
                total = total + bufs["b2r"][j, there].astype(f32)
            if k < 3:
                bufs["b3s"][k] = total.astype(bf16)
                third_b.append(send(bufs["b3s"].at[k], bufs["b3r"].at[k], sem, 22 + k, along("x", k + 1)))
            else:
                mine_b = total
        for k in range(3):
            third_a[k].wait_recv()
            mine_a = mine_a + bufs["a3r"][k].astype(f32)
        bufs["shard"][:h, :] = mine_a
        for k in range(3):
            third_b[k].wait_recv()
            mine_b = mine_b + bufs["b3r"][k].astype(f32)
        bufs["shard"][h:, :] = mine_b
        flush()

    def gram_steps(bufs):
        part = bufs["shard"][...]
        gram_own[...] = lax.dot_general(
            part, part, (((0,), (0,)), ((), ())), precision=HIGHEST, preferred_element_type=f32
        )
        h = K // 2
        mine = pl.ds(pl.multiple_of(c * h, h), h)
        theirs = pl.ds(pl.multiple_of((1 - c) * h, h), h)
        copy = send(gram_own.at[theirs, :], gram_first, gram_sem, 0, along("core", 0))
        yield
        copy.wait_recv()
        total = gram_own[mine, :] + gram_first[...]
        for stage, (axis, place) in enumerate((("x", x), ("z", z), ("y", y))):
            gram_slots[stage, place] = total
            copies = [
                send(gram_slots.at[stage, place], gram_slots.at[stage, place], gram_sem, 1 + 3 * stage + j - 1, along(axis, j))
                for j in (1, 2, 3)
            ]
            yield
            for copy in copies:
                copy.wait_recv()
            total = gram_slots[stage, 0] + gram_slots[stage, 1] + gram_slots[stage, 2] + gram_slots[stage, 3]
        gram_half[...] = total
        gram_all[mine, :] = total
        copy = send(gram_half, gram_all.at[mine, :], gram_sem, 10, along("core", 0))
        yield
        copy.wait_recv()
        yield

    def factor_from_gram(row_total, out):
        g = gram_all[...]
        i = lax.broadcasted_iota(jnp.int32, (K, K), 0)
        j = lax.broadcasted_iota(jnp.int32, (K, K), 1)
        on_diagonal = jnp.where(i == j, g, 0.0)
        shift = 1e-5 * jnp.sum(jnp.sum(on_diagonal, axis=1, keepdims=True), axis=0, keepdims=True) / K
        out[...] = inverse_factor(g + jnp.where(i == j, shift, 0.0)) * f32(row_total**0.5)

    def gather_panel(bufs, steps):
        g, sem, shard = bufs["gathered"], bufs["sem"], bufs["shard"]
        h = shard.shape[0] // 2
        g[z, x, c] = shard[...].astype(bf16)
        top, bottom = pl.ds(0, h), pl.ds(h, h)

        def piece(z_, x_, part):
            return g.at[z_, x_, c, part, :]

        base = 25
        a1 = [send(piece(z, x, top), piece(z, x, top), sem, base + j - 1, along("z", j)) for j in (1, 2, 3)]
        b1 = [send(piece(z, x, bottom), piece(z, x, bottom), sem, base + 3 + j - 1, along("x", j)) for j in (1, 2, 3)]
        a2, b2 = {}, {}

        def forward(k):
            from_z, from_x = lax.rem(z - k + SIDE, SIDE), lax.rem(x - k + SIDE, SIDE)
            for j in (1, 2, 3):
                a2[k, j] = send(
                    piece(from_z, x, top), piece(from_z, x, top), sem, base + 6 + k * 3 + j - 1, along("x", j)
                )
                b2[k, j] = send(
                    piece(z, from_x, bottom), piece(z, from_x, bottom), sem, base + 18 + k * 3 + j - 1, along("z", j)
                )

        forward(0)
        next(steps)
        for k in (1, 2, 3):
            a1[k - 1].wait_recv()
            b1[k - 1].wait_recv()
            forward(k)
        cores = []

        def over(ref):
            cores.append(send(ref, ref, sem, base + 30 + len(cores), along("core", 0)))

        over(g.at[:, x, c, top, :])
        over(g.at[z, :, c, bottom, :])
        next(steps)
        for j in (1, 2, 3):
            for k in range(SIDE):
                a2[k, j].wait_recv()
            over(g.at[:, lax.rem(x - j + SIDE, SIDE), c, top, :])
            for k in range(SIDE):
                b2[k, j].wait_recv()
            over(g.at[lax.rem(z - j + SIDE, SIDE), :, c, bottom, :])
            if j < 3:
                next(steps)
        for copy in cores:
            copy.wait_recv()

    row_y, row_z = float(SIDE * features), float(SIDE * hidden)
    for iteration in range(ITERS):
        sends = []
        if iteration == 0:
            loads[0].wait()
            for k in range(SIDE):
                span = pl.ds(pl.multiple_of(turn[k] * tokens, tokens), tokens)
                loads[1 + k].wait()
                s_part[span, :] = jnp.zeros((tokens, K), f32)

                @pl.loop(0, SIDE)
                def _(i):
                    deep = pl.ds(pl.multiple_of(i * (hidden // SIDE), K), hidden // SIDE)
                    s_part[span, :] += jnp.dot(o[span, deep], sketch[deep, :], preferred_element_type=f32)

                if k < 3:
                    sends.append(send_tokens(k))
            loads[5].wait()
            share_tokens(sends, None)
        else:
            s_part[...] = jnp.zeros(s_part.shape, f32)
            n = hidden // SIDE

            @pl.loop(0, SIDE)
            def _(i):
                deep = pl.ds(pl.multiple_of(i * n, K), n)
                block = bufs_z["gathered"][i].reshape(n, K)
                s_part[...] += jnp.dot(o[:, deep], block, preferred_element_type=f32)

            sends = [send_tokens(k) for k in range(3)]
            for _ in steps:
                pass
            factor_from_gram(row_z, factor_z)
            share_tokens(sends, lambda: factor_z[...])
        reduce_panel(a, bufs_y, features)
        steps = gram_steps(bufs_y)
        gather_panel(bufs_y, steps)
        s_part[...] = jnp.dot(a[...], bufs_y["gathered"][...].reshape(features, K), preferred_element_type=f32)
        sends = [send_tokens(k) for k in range(3)]
        for _ in steps:
            pass
        factor_from_gram(row_y, factor_y)
        share_tokens(sends, lambda: factor_y[...])
        if iteration == ITERS - 1:
            q = lax.dot_general(
                bufs_y["shard"][...], factor_y[...], (((1,), (1,)), ((), ())), precision=HIGHEST, preferred_element_type=f32
            )
            q_ref[...] = q[:, :RANK]
        reduce_panel(o, bufs_z, hidden)
        steps = gram_steps(bufs_z)
        if iteration < ITERS - 1:
            gather_panel(bufs_z, steps)
    for _ in steps:
        pass
    factor_from_gram(row_z, factor_z)
    p = lax.dot_general(
        bufs_z["shard"][...], factor_z[...], (((1,), (1,)), ((), ())), precision=HIGHEST, preferred_element_type=f32
    )
    p_ref[...] = p[:, RANK:]
    flush()


def panel_scratch(rows):
    h = rows // 2
    return [
        pltpu.VMEM((4, 4, rows, K), f32),
        pltpu.VMEM((4, 4, rows, K), bf16),
        pltpu.VMEM((4, 4, rows, K), bf16),
        pltpu.VMEM((4, 4, h, K), bf16),
        pltpu.VMEM((4, 3, h, K), bf16),
        pltpu.VMEM((4, 4, h, K), bf16),
        pltpu.VMEM((3, 4, h, K), bf16),
        pltpu.VMEM((3, h, K), bf16),
        pltpu.VMEM((3, h, K), bf16),
        pltpu.VMEM((3, h, K), bf16),
        pltpu.VMEM((3, h, K), bf16),
        pltpu.VMEM((rows, K), f32),
        pltpu.VMEM((4, 4, 2, rows, K), bf16),
        pltpu.SemaphoreType.DMA((2, 64)),
    ]


def body(activations, out_grads, sketch):
    tokens, features = activations.shape
    hidden = out_grads.shape[1]
    devices = lax.axis_size("dp")
    rows_y, rows_z = features // devices, hidden // devices
    quarter = tokens // SIDE
    scratch = [
        pltpu.VMEM((tokens, features), bf16),
        pltpu.VMEM((tokens, hidden), bf16),
        pltpu.VMEM((hidden, K), bf16),
        pltpu.SemaphoreType.DMA((6,)),
        pltpu.VMEM((tokens, K), f32),
        pltpu.VMEM((3, quarter, K), f32),
        pltpu.VMEM((quarter, K), bf16),
        pltpu.VMEM((tokens, K), bf16),
        pltpu.VMEM((K, tokens), bf16),
        pltpu.SemaphoreType.DMA((2, 6)),
        pltpu.VMEM((K, K), f32),
        pltpu.VMEM((K // 2, K), f32),
        pltpu.VMEM((3, SIDE, K // 2, K), f32),
        pltpu.VMEM((K // 2, K), f32),
        pltpu.VMEM((K, K), f32),
        pltpu.SemaphoreType.DMA((2, 11)),
        pltpu.VMEM((K, K), f32),
        pltpu.VMEM((K, K), f32),
        *panel_scratch(rows_y),
        *panel_scratch(rows_z),
    ]
    return pl.pallas_call(
        functools.partial(kernel, features, hidden),
        out_shape=(
            jax.ShapeDtypeStruct((rows_y, RANK), f32),
            jax.ShapeDtypeStruct((rows_z, K - RANK), f32),
        ),
        in_specs=[pl.BlockSpec(memory_space=pl.ANY)] * 3,
        out_specs=(pl.BlockSpec(memory_space=pltpu.VMEM), pl.BlockSpec(memory_space=pltpu.VMEM)),
        scratch_shapes=scratch,
        compiler_params=pltpu.CompilerParams(
            collective_id=0, has_side_effects=True, vmem_limit_bytes=58 << 20
        ),
        name="subspace_iteration",
    )(activations, out_grads, sketch)


def solution(mesh):
    return jax.shard_map(
        body,
        mesh=mesh,
        in_specs=(P("dp", "col"), P("dp", "col"), P("col", None)),
        out_specs=(P(("col", "dp"), None), P(("col", "dp"), None)),
        check_vma=False,
    )
```

time: 813 us -> 201 us (0.25); the launches traced: 802 us -> 201 us
  waiting for transfers between devices: 366 us -> 0 us
  Pallas kernels: 0 us -> 197 us
  blocking collectives: 197 us -> 0 us
  matrix products: 107 us -> 0 us
  other arithmetic: 103 us -> 0 us
  between operations: 17.2 us -> 0.64 us
    psum x2 -> x0, waiting for transfers between devices: 228 us -> none  [body(): right_full = lax.psum(whole_part, 'dp')]
    pallas_call x0 -> x1, Pallas kernels: none -> 197 us  [body(): pl.pallas_call(functools.partial(kernel, features, hidden), out_shape=(ja...]
    all_to_all x9 -> x0, blocking collectives: 197 us -> none  [the longest x7 121 us: copy_for_each(): lax.all_to_all(jnp.broadcast_to(x[None], (count, *x.shape)), axis, 0, 0,...]
    all_gather x2 -> x0, waiting for transfers between devices: 132 us -> none  [total_of_pieces(): return lax.all_gather(x, axis).sum(0)]
    dot_general x16 -> x0, matrix products: 106 us -> none  [the longest x4 36.4 us: cholesky_basis(): jnp.dot(panel_in, inverse.T, precision=lax.Precision.HIGHEST, preferred_e...]
    another operation x20 -> x0, other arithmetic: 91.4 us -> none  [the longest x12 49.6 us: cholesky_basis(): lower_factor = jnp.linalg.cholesky(gram_matrix + shift_value * identity_k)]
    reduce_sum x14 -> x0, other arithmetic: 10.6 us -> none  [the longest x2 7.61 us: total_of_pieces(): return lax.all_gather(x, axis).sum(0)]
  transfers between devices with their start and end apart: 5 -> 0, of which waited for: 5 -> 0; matrix products, arithmetic and copies ran while one was open for 0% -> 0% of each run, Pallas kernels for 0% -> 0%
where the time goes in v1:
time: 201 us
  Pallas kernels  197 us (98%)
  local copies, waits for them, and re-layouts  3.24 us (2%)
    pallas_call x1, Pallas kernels, body(): pl.pallas_call(functools.partial(kernel, features, hidden), out_shape=(ja...  197 us

profile of v1, /device:TPU:1, one launch (start us, length us, event | category | flops | bytes accessed | tf_op | source)
XLA Modules:
  0.0 201.3 jit_solution(10649996769074025117)
XLA Ops:
  0.6 197.4 %subspace_iteration.1 = (f32[128,64]{1,0:T(8,128)}, f32[416,64]{1,0:T(8,128)}) custom-call(bf16[512,4096]{1,0:T(8,128)(2,1)} %a_hbm.1, bf16[512,13312]{1,0:T(8,128)(2,1)} %o_hbm.1, bf16[13312,128]{1,0:T(8,128)(2,1)} %sk_hbm.1), custom_call_target="tpu_custom_call" | custom-call | tf_op jit(solution)/shard_map/subspace_iteration/pallas_call | solution.py:430
  198.0 1.5 copy.5
  199.6 1.7 copy.6

commit v2 on v1

v2 whole, which is shorter than its diff:
```python
import functools

import jax
import jax.numpy as jnp
from jax import lax
from jax.experimental import pallas as pl
from jax.experimental.pallas import tpu as pltpu
from jax.sharding import PartitionSpec as P

RANK = 64
ITERS = 2
K = 128
f32 = jnp.float32
bf16 = jnp.bfloat16
HIGHEST = lax.Precision.HIGHEST
SIDE = 4


def lanes_of(x, k):
    return jnp.broadcast_to(x[:, k : k + 1], (8, K))


def row_of(x, k):
    return jnp.broadcast_to(x[k : k + 1, :], (8, K))


def inverse_factor(matrix):
    lane = lax.broadcasted_iota(jnp.int32, (8, K), 1)
    sub = lax.broadcasted_iota(jnp.int32, (8, K), 0)
    rows = [matrix[8 * u : 8 * u + 8, :] for u in range(16)]
    for b in range(16):
        first = 8 * b
        inside = (lane >= first) & (lane < first + 8)
        pivots = [lanes_of(rows[b], first + k) for k in range(8)]
        panel = jnp.where(inside, jnp.where(lane == sub + first, 1.0, 0.0), rows[b])
        recip, coef, done = [], {}, []
        scale = jnp.zeros((8, K), f32)
        for k in range(8):
            d = row_of(pivots[k], k)
            recip.append(1.0 / d)
            scale = jnp.where(sub == k, lax.rsqrt(d), scale)
            done.append(row_of(panel, k))
            if k < 7:
                c = jnp.where(sub > k, pivots[k] * recip[k], 0.0)
                for m in range(k + 1, 8):
                    coef[k, m] = row_of(pivots[m], k)
                    pivots[m] = pivots[m] - c * coef[k, m]
                panel = panel - c * done[k]
        rows[b] = panel * scale
        for u in range(b + 1, 16):
            cols = [lanes_of(rows[u], first + k) for k in range(8)]
            acc = jnp.where(inside, 0.0, rows[u])
            for k in range(8):
                ck = cols[k] * recip[k]
                for m in range(k + 1, 8):
                    cols[m] = cols[m] - ck * coef[k, m]
                acc = acc - ck * done[k]
            rows[u] = acc
    whole = jnp.concatenate(rows, axis=0)
    i = lax.broadcasted_iota(jnp.int32, (K, K), 0)
    j = lax.broadcasted_iota(jnp.int32, (K, K), 1)
    return jnp.where(j <= i, whole, 0.0)


def wave_rows(rows):
    tiles = rows // 16
    counts = [tiles // 4 + (1 if tiles % 4 > i else 0) for i in (0, 2, 3, 1)]
    spans, first = [], 0
    for count in counts:
        spans.append((first, count * 16))
        first += count * 16
    return (spans[0], spans[1]), (spans[2], spans[3])


def kernel(
    features, hidden, a_hbm, o_hbm, sk_hbm, q_ref, p_ref,
    a, o, sketch, load_sem,
    s_part, s_recv, s_mine, s_all, s_t, s_sem,
    gram_own, gram_first, gram_slots, gram_half, gram_all, gram_sem, factor_y, factor_z,
    *panel_refs,
):
    dp, y = lax.axis_index("dp"), lax.axis_index("col")
    z, x, c = dp // 8, lax.rem(dp // 2, SIDE), lax.rem(dp, 2)
    names = ("own", "c1s", "c1r", "s2", "a2r", "b2r", "s3", "r3", "shard", "gathered", "sem")
    half = len(names)
    bufs_y = dict(zip(names, panel_refs[:half]))
    bufs_z = dict(zip(names, panel_refs[half:]))

    def at(z_=None, x_=None, c_=None):
        z_ = z if z_ is None else z_
        x_ = x if x_ is None else x_
        c_ = c if c_ is None else c_
        return {"dp": (z_ * SIDE + x_) * 2 + c_, "col": y}

    def along(axis, j):
        if axis == "x":
            return at(x_=lax.rem(x + j, SIDE))
        if axis == "z":
            return at(z_=lax.rem(z + j, SIDE))
        if axis == "y":
            return {"dp": dp, "col": lax.rem(y + j, SIDE)}
        return at(c_=1 - c)

    pending = []

    def send(src, dst, sems, index, device):
        copy = pltpu.make_async_remote_copy(
            src_ref=src, dst_ref=dst, send_sem=sems.at[0, index], recv_sem=sems.at[1, index],
            device_id=device, device_id_type=pl.DeviceIdType.MESH,
        )
        copy.start()
        pending.append(copy)
        return copy

    def flush():
        for copy in pending:
            copy.wait_send()
        pending.clear()

    barrier = pltpu.get_barrier_semaphore()
    partners = [along("core", 0)] + [along(axis, j) for axis in "xyz" for j in (1, 2, 3)]
    for device in partners:
        pl.semaphore_signal(barrier, inc=1, device_id=device, device_id_type=pl.DeviceIdType.MESH)

    tokens = s_mine.shape[0]
    turn = [lax.rem(y + 1 + k, SIDE) for k in range(SIDE)]
    loads = [pltpu.make_async_copy(sk_hbm, sketch, load_sem.at[0])]
    for k in range(SIDE):
        span = pl.ds(pl.multiple_of(turn[k] * tokens, tokens), tokens)
        loads.append(pltpu.make_async_copy(o_hbm.at[span, :], o.at[span, :], load_sem.at[1 + k]))
    loads.append(pltpu.make_async_copy(a_hbm, a, load_sem.at[5]))
    for copy in loads:
        copy.start()

    def send_tokens(k):
        span = pl.ds(pl.multiple_of(turn[k] * tokens, tokens), tokens)
        return send(s_part.at[span, :], s_recv.at[k], s_sem, k, along("y", k + 1))

    def share_tokens(sends, factor):
        span = pl.ds(pl.multiple_of(y * tokens, tokens), tokens)
        total = s_part[span, :]
        for k in range(3):
            sends[k].wait_recv()
            total = total + s_recv[k]
        if factor is not None:
            total = lax.dot_general(
                total, factor(), (((1,), (1,)), ((), ())), precision=HIGHEST, preferred_element_type=f32
            )
        s_all[span, :] = total.astype(bf16)
        outs = [send(s_all.at[span, :], s_all.at[span, :], s_sem, 3 + k, along("y", k + 1)) for k in range(3)]
        for copy in outs:
            copy.wait_recv()
        flush()
        s_t[...] = s_all[...].T

    def gram_steps(bufs):
        part = bufs["shard"][...]
        gram_own[...] = lax.dot_general(
            part, part, (((0,), (0,)), ((), ())), precision=HIGHEST, preferred_element_type=f32
        )
        h = K // 2
        mine = pl.ds(pl.multiple_of(c * h, h), h)
        theirs = pl.ds(pl.multiple_of((1 - c) * h, h), h)
        copy = send(gram_own.at[theirs, :], gram_first, gram_sem, 0, along("core", 0))
        yield
        copy.wait_recv()
        total = gram_own[mine, :] + gram_first[...]
        thirds = ((0, 24, "xzy"), (24, 24, "zyx"), (48, 16, "yxz"))
        places = {"x": x, "z": z, "y": y}
        totals = [total[first : first + count] for first, count, _ in thirds]
        for stage in range(3):
            copies = []
            for part, (first, count, order) in enumerate(thirds):
                span, place = pl.ds(first, count), places[order[stage]]
                gram_slots[stage, place, span, :] = totals[part]
                for j in (1, 2, 3):
                    ref = gram_slots.at[stage, place, span, :]
                    copies.append(send(ref, ref, gram_sem, 2 + 9 * stage + 3 * part + j - 1, along(order[stage], j)))
            yield
            for part, (first, count, order) in enumerate(thirds):
                for copy in copies[3 * part : 3 * part + 3]:
                    copy.wait_recv()
                terms = [gram_slots[stage, i, first : first + count, :] for i in range(SIDE)]
                totals[part] = terms[0] + terms[1] + terms[2] + terms[3]
        total = jnp.concatenate(totals, axis=0)
        gram_half[...] = total
        gram_all[mine, :] = total
        copy = send(gram_half, gram_all.at[mine, :], gram_sem, 1, along("core", 0))
        yield
        copy.wait_recv()
        yield

    def factor_from_gram(row_total, out):
        g = gram_all[...]
        i = lax.broadcasted_iota(jnp.int32, (K, K), 0)
        j = lax.broadcasted_iota(jnp.int32, (K, K), 1)
        on_diagonal = jnp.where(i == j, g, 0.0)
        shift = 1e-5 * jnp.sum(jnp.sum(on_diagonal, axis=1, keepdims=True), axis=0, keepdims=True) / K
        out[...] = inverse_factor(g + jnp.where(i == j, shift, 0.0)) * f32(row_total**0.5)

    def pass_panel(weights, bufs, columns, gather):
        own, c1s, c1r, s2, sem = bufs["own"], bufs["c1s"], bufs["c1r"], bufs["s2"], bufs["sem"]
        a2r, b2r, s3, r3, shard, g = bufs["a2r"], bufs["b2r"], bufs["s3"], bufs["r3"], bufs["shard"], bufs["gathered"]
        rows = own.shape[2]
        waves = wave_rows(rows)
        zs = [lax.rem(z + 1 + k, SIDE) for k in range(SIDE)]
        span = columns // SIDE
        pieces = 1 if span % 1024 == 0 else 2
        first = []

        def compute(k):
            for piece in range(pieces):
                width = span // pieces
                n = SIDE // pieces
                start = pl.multiple_of(zs[k] * span + piece * width, K)
                r = jnp.dot(s_t[...], weights[:, pl.ds(start, width)], preferred_element_type=f32).T
                r = r.reshape(n, 2, rows, K)
                own[k, piece * n : (piece + 1) * n] = jnp.where(c == 0, r[:, 0], r[:, 1])
                c1s[k, piece * n : (piece + 1) * n] = jnp.where(c == 0, r[:, 1], r[:, 0]).astype(bf16)
            first.append(send(c1s.at[k], c1r.at[k], sem, k, along("core", 0)))

        def add_core(k):
            first[k].wait_recv()
            for i in range(SIDE):
                v = own[k, i] + c1r[k, i].astype(f32)
                own[k, i] = v
                s2[k, i] = v.astype(bf16)

        class Wave:
            def __init__(self, index):
                self.a, self.b = waves[index]
                self.base = 4 + 59 * index
                self.second_a, self.second_b, self.third_a, self.third_b = [], [], [], []
                self.gather_a, self.gather_b, self.on_a, self.on_b, self.cores = [], [], {}, {}, []

            def second(self, k):
                for j in (1, 2, 3):
                    there = lax.rem(x + j, SIDE)
                    self.second_a.append(
                        send(
                            s2.at[k, there, pl.ds(*self.a), :], a2r.at[k, j - 1, pl.ds(*self.a), :],
                            sem, self.base + k * 3 + j - 1, along("x", j),
                        )
                    )
                if k < 3:
                    self.second_b.append(
                        send(
                            s2.at[k, :, pl.ds(*self.b), :], b2r.at[k, :, pl.ds(*self.b), :],
                            sem, self.base + 12 + k, along("z", k + 1),
                        )
                    )

            def third(self):
                part = pl.ds(*self.a)
                for k in range(SIDE):
                    total = own[k, x, part, :]
                    for j in range(3):
                        self.second_a[k * 3 + j].wait_recv()
                        total = total + a2r[k, j, part, :].astype(f32)
                    if k < 3:
                        s3[k, part, :] = total.astype(bf16)
                        self.third_a.append(
                            send(s3.at[k, part, :], r3.at[k, part, :], sem, self.base + 15 + k, along("z", k + 1))
                        )
                    else:
                        shard[part, :] = total
                part = pl.ds(*self.b)
                for k in range(3):
                    self.second_b[k].wait_recv()
                for k in range(SIDE):
                    there = lax.rem(x + 1 + k, SIDE)
                    total = own[3, there, part, :]
                    for j in range(3):
                        total = total + b2r[j, there, part, :].astype(f32)
                    if k < 3:
                        s3[k, part, :] = total.astype(bf16)
                        self.third_b.append(
                            send(s3.at[k, part, :], r3.at[k, part, :], sem, self.base + 18 + k, along("x", k + 1))
                        )
                    else:
                        shard[part, :] = total

            def piece(self, z_, x_, part):
                return g.at[z_, x_, c, pl.ds(*part), :]

            def finish(self):
                for part, copies in ((self.a, self.third_a), (self.b, self.third_b)):
                    part = pl.ds(*part)
                    total = shard[part, :]
                    for k in range(3):
                        copies[k].wait_recv()
                        total = total + r3[k, part, :].astype(f32)
                    shard[part, :] = total
                    if gather:
                        g[z, x, c, part, :] = total.astype(bf16)
                        axis, part, base, outs = (
                            ("z", self.a, 21, self.gather_a) if copies is self.third_a else ("x", self.b, 24, self.gather_b)
                        )
                        for j in (1, 2, 3):
                            ref = self.piece(z, x, part)
                            outs.append(send(ref, ref, sem, self.base + base + j - 1, along(axis, j)))
                if gather:
                    self.forward(0)

            def forward(self, k):
                if k > 0:
                    self.gather_a[k - 1].wait_recv()
                    self.gather_b[k - 1].wait_recv()
                from_z, from_x = lax.rem(z - k + SIDE, SIDE), lax.rem(x - k + SIDE, SIDE)
                for j in (1, 2, 3):
                    ref = self.piece(from_z, x, self.a)
                    self.on_a[k, j] = send(ref, ref, sem, self.base + 27 + k * 3 + j - 1, along("x", j))
                    ref = self.piece(z, from_x, self.b)
                    self.on_b[k, j] = send(ref, ref, sem, self.base + 39 + k * 3 + j - 1, along("z", j))

            def over(self, ref):
                self.cores.append(send(ref, ref, sem, self.base + 51 + len(self.cores), along("core", 0)))

            def first_hop(self):
                for k in (1, 2, 3):
                    self.forward(k)
                self.over(g.at[:, x, c, pl.ds(*self.a), :])
                self.over(g.at[z, :, c, pl.ds(*self.b), :])

            def second_hop(self):
                for j in (1, 2, 3):
                    for k in range(SIDE):
                        self.on_a[k, j].wait_recv()
                    self.over(g.at[:, lax.rem(x - j + SIDE, SIDE), c, pl.ds(*self.a), :])
                    for k in range(SIDE):
                        self.on_b[k, j].wait_recv()
                    self.over(g.at[lax.rem(z - j + SIDE, SIDE), :, c, pl.ds(*self.b), :])

            def wait_cores(self):
                for copy in self.cores:
                    copy.wait_recv()

        one, two = Wave(0), Wave(1)
        for k in range(SIDE):
            compute(k)
            if k > 0:
                add_core(k - 1)
                one.second(k - 1)
        add_core(3)
        one.second(3)
        for k in range(SIDE):
            two.second(k)
        one.third()
        if rows > 256:
            one.finish()
            two.third()
        else:
            two.third()
            one.finish()
        if gather and rows > 256:
            one.first_hop()
        two.finish()
        steps = gram_steps(bufs)
        if not gather:
            return steps
        next(steps)
        next(steps)
        if rows <= 256:
            one.first_hop()
        two.first_hop()
        next(steps)
        one.second_hop()
        two.second_hop()
        next(steps)
        one.wait_cores()
        two.wait_cores()
        return steps

    row_y, row_z = float(SIDE * features), float(SIDE * hidden)
    for iteration in range(ITERS):
        sends = []
        if iteration == 0:
            loads[0].wait()
            for k in range(SIDE):
                span = pl.ds(pl.multiple_of(turn[k] * tokens, tokens), tokens)
                loads[1 + k].wait()
                s_part[span, :] = jnp.zeros((tokens, K), f32)

                @pl.loop(0, SIDE)
                def _(i):
                    deep = pl.ds(pl.multiple_of(i * (hidden // SIDE), K), hidden // SIDE)
                    s_part[span, :] += jnp.dot(o[span, deep], sketch[deep, :], preferred_element_type=f32)

                if k == 0:
                    pl.semaphore_wait(barrier, len(partners))
                if k < 3:
                    sends.append(send_tokens(k))
            loads[5].wait()
            share_tokens(sends, None)
        else:
            s_part[...] = jnp.zeros(s_part.shape, f32)
            n = hidden // SIDE

            @pl.loop(0, SIDE)
            def _(i):
                deep = pl.ds(pl.multiple_of(i * n, K), n)
                block = bufs_z["gathered"][i].reshape(n, K)
                s_part[...] += jnp.dot(o[:, deep], block, preferred_element_type=f32)

            sends = [send_tokens(k) for k in range(3)]
            for _ in steps:
                pass
            factor_from_gram(row_z, factor_z)
            share_tokens(sends, lambda: factor_z[...])
        steps = pass_panel(a, bufs_y, features, True)
        s_part[...] = jnp.dot(a[...], bufs_y["gathered"][...].reshape(features, K), preferred_element_type=f32)
        sends = [send_tokens(k) for k in range(3)]
        for _ in steps:
            pass
        factor_from_gram(row_y, factor_y)
        share_tokens(sends, lambda: factor_y[...])
        if iteration == ITERS - 1:
            q = lax.dot_general(
                factor_y[...], bufs_y["shard"][...], (((1,), (1,)), ((), ())), precision=HIGHEST, preferred_element_type=f32
            )
            q_ref[...] = q[:RANK, :]
        steps = pass_panel(o, bufs_z, hidden, iteration < ITERS - 1)
    for _ in steps:
        pass
    factor_from_gram(row_z, factor_z)
    p = lax.dot_general(
        factor_z[...], bufs_z["shard"][...], (((1,), (1,)), ((), ())), precision=HIGHEST, preferred_element_type=f32
    )
    p_ref[...] = p[RANK:, :]
    flush()


def panel_scratch(rows):
    return [
        pltpu.VMEM((4, 4, rows, K), f32),
        pltpu.VMEM((4, 4, rows, K), bf16),
        pltpu.VMEM((4, 4, rows, K), bf16),
        pltpu.VMEM((4, 4, rows, K), bf16),
        pltpu.VMEM((4, 3, rows, K), bf16),
        pltpu.VMEM((3, 4, rows, K), bf16),
        pltpu.VMEM((3, rows, K), bf16),
        pltpu.VMEM((3, rows, K), bf16),
        pltpu.VMEM((rows, K), f32),
        pltpu.VMEM((4, 4, 2, rows, K), bf16),
        pltpu.SemaphoreType.DMA((2, 122)),
    ]


def body(activations, out_grads, sketch):
    tokens, features = activations.shape
    hidden = out_grads.shape[1]
    devices = lax.axis_size("dp")
    rows_y, rows_z = features // devices, hidden // devices
    quarter = tokens // SIDE
    scratch = [
        pltpu.VMEM((tokens, features), bf16),
        pltpu.VMEM((tokens, hidden), bf16),
        pltpu.VMEM((hidden, K), bf16),
        pltpu.SemaphoreType.DMA((6,)),
        pltpu.VMEM((tokens, K), f32),
        pltpu.VMEM((3, quarter, K), f32),
        pltpu.VMEM((quarter, K), bf16),
        pltpu.VMEM((tokens, K), bf16),
        pltpu.VMEM((K, tokens), bf16),
        pltpu.SemaphoreType.DMA((2, 6)),
        pltpu.VMEM((K, K), f32),
        pltpu.VMEM((K // 2, K), f32),
        pltpu.VMEM((3, SIDE, K // 2, K), f32),
        pltpu.VMEM((K // 2, K), f32),
        pltpu.VMEM((K, K), f32),
        pltpu.SemaphoreType.DMA((2, 29)),
        pltpu.VMEM((K, K), f32),
        pltpu.VMEM((K, K), f32),
        *panel_scratch(rows_y),
        *panel_scratch(rows_z),
    ]
    q, p = pl.pallas_call(
        functools.partial(kernel, features, hidden),
        out_shape=(
            jax.ShapeDtypeStruct((RANK, rows_y), f32),
            jax.ShapeDtypeStruct((K - RANK, rows_z), f32),
        ),
        in_specs=[pl.BlockSpec(memory_space=pl.ANY)] * 3,
        out_specs=(pl.BlockSpec(memory_space=pltpu.VMEM), pl.BlockSpec(memory_space=pltpu.VMEM)),
        scratch_shapes=scratch,
        compiler_params=pltpu.CompilerParams(
            collective_id=0, has_side_effects=True, vmem_limit_bytes=58 << 20
        ),
        name="subspace_iteration",
    )(activations, out_grads, sketch)
    return q.T, p.T


def solution(mesh):
    return jax.shard_map(
        body,
        mesh=mesh,
        in_specs=(P("dp", "col"), P("dp", "col"), P("col", None)),
        out_specs=(P(("col", "dp"), None), P(("col", "dp"), None)),
        check_vma=False,
    )
```

time: 201 us -> 184 us (0.915)
  Pallas kernels: 197 us -> 180 us
    pallas_call x1, Pallas kernels: 197 us -> 180 us  [body(): pl.pallas_call(functools.partial(kernel, features, hidden), out_shape=(ja...]
    pallas_call x2 -> x0, local copies, waits for them, and re-layouts: 3.24 us -> none  [body(): pl.pallas_call(functools.partial(kernel, features, hidden), out_shape=(ja...]
    unnamed x0 -> x2, local copies, waits for them, and re-layouts: none -> 2.94 us
where the time goes in v2:
time: 184 us
  Pallas kernels  180 us (98%)
  local copies, waits for them, and re-layouts  2.94 us (2%)
    pallas_call x1, Pallas kernels, body(): pl.pallas_call(functools.partial(kernel, features, hidden), out_shape=(ja...  180 us

profile of v2, /device:TPU:1, one launch (start us, length us, event | category | flops | bytes accessed | tf_op | source)
XLA Modules:
  0.0 183.6 jit_solution(7960927045715455690)
XLA Ops:
  0.6 180.0 %subspace_iteration.1 = (f32[64,128]{1,0:T(8,128)}, f32[64,416]{1,0:T(8,128)}) custom-call(bf16[512,4096]{1,0:T(8,128)(2,1)} %a_hbm.1, bf16[512,13312]{1,0:T(8,128)(2,1)} %o_hbm.1, bf16[13312,128]{1,0:T(8,128)(2,1)} %sk_hbm.1), custom_call_target="tpu_custom_call" | custom-call | tf_op jit(solution)/shard_map/subspace_iteration/pallas_call | solution.py:477
  180.6 1.4 copy.7
  182.0 1.6 copy.8

commit v3 on v2

--- a/solution.py
+++ b/solution.py
@@ -14,6 +14,7 @@
 bf16 = jnp.bfloat16
 HIGHEST = lax.Precision.HIGHEST
 SIDE = 4
+HOPS = (2, 1, 3)
 
 
 def lanes_of(x, k):
@@ -123,22 +124,24 @@
         pl.semaphore_signal(barrier, inc=1, device_id=device, device_id_type=pl.DeviceIdType.MESH)
 
     tokens = s_mine.shape[0]
-    turn = [lax.rem(y + 1 + k, SIDE) for k in range(SIDE)]
+
+    def quarter(k, count=1):
+        return pl.ds(k * tokens, count * tokens)
+
+    turn = [lax.rem(y + hop, SIDE) for hop in (*HOPS, 0)]
     loads = [pltpu.make_async_copy(sk_hbm, sketch, load_sem.at[0])]
-    for k in range(SIDE):
-        span = pl.ds(pl.multiple_of(turn[k] * tokens, tokens), tokens)
-        loads.append(pltpu.make_async_copy(o_hbm.at[span, :], o.at[span, :], load_sem.at[1 + k]))
-    loads.append(pltpu.make_async_copy(a_hbm, a, load_sem.at[5]))
+    for held, source, sem in ((o, o_hbm, 1), (a, a_hbm, 5)):
+        for k in range(SIDE):
+            span = pl.ds(pl.multiple_of(turn[k] * tokens, tokens), tokens)
+            loads.append(pltpu.make_async_copy(source.at[span, :], held.at[quarter(k), :], load_sem.at[sem + k]))
     for copy in loads:
         copy.start()
 
     def send_tokens(k):
-        span = pl.ds(pl.multiple_of(turn[k] * tokens, tokens), tokens)
-        return send(s_part.at[span, :], s_recv.at[k], s_sem, k, along("y", k + 1))
+        return send(s_part.at[quarter(k), :], s_recv.at[k], s_sem, k, along("y", HOPS[k]))
 
     def share_tokens(sends, factor):
-        span = pl.ds(pl.multiple_of(y * tokens, tokens), tokens)
-        total = s_part[span, :]
+        total = s_part[quarter(3), :]
         for k in range(3):
             sends[k].wait_recv()
             total = total + s_recv[k]
@@ -146,18 +149,27 @@
             total = lax.dot_general(
                 total, factor(), (((1,), (1,)), ((), ())), precision=HIGHEST, preferred_element_type=f32
             )
-        s_all[span, :] = total.astype(bf16)
-        outs = [send(s_all.at[span, :], s_all.at[span, :], s_sem, 3 + k, along("y", k + 1)) for k in range(3)]
-        for copy in outs:
+        s_all[quarter(3), :] = total.astype(bf16)
+        outs = [
+            send(
+                s_all.at[quarter(3), :], s_all.at[quarter(HOPS.index(SIDE - hop)), :], s_sem, 3 + k, along("y", hop)
+            )
+            for k, hop in enumerate(HOPS)
+        ]
+        s_t[:, quarter(3)] = s_all[quarter(3), :].T
+        for copy, hop in zip(outs, HOPS):
             copy.wait_recv()
+            came = quarter(HOPS.index(SIDE - hop))
+            s_t[:, came] = s_all[came, :].T
         flush()
-        s_t[...] = s_all[...].T
-
-    def gram_steps(bufs):
-        part = bufs["shard"][...]
-        gram_own[...] = lax.dot_general(
+
+    def local_gram(bufs, first, count):
+        part = bufs["shard"][first : first + count, :]
+        return lax.dot_general(
             part, part, (((0,), (0,)), ((), ())), precision=HIGHEST, preferred_element_type=f32
         )
+
+    def gram_steps():
         h = K // 2
         mine = pl.ds(pl.multiple_of(c * h, h), h)
         theirs = pl.ds(pl.multiple_of((1 - c) * h, h), h)
@@ -173,7 +185,7 @@
             for part, (first, count, order) in enumerate(thirds):
                 span, place = pl.ds(first, count), places[order[stage]]
                 gram_slots[stage, place, span, :] = totals[part]
-                for j in (1, 2, 3):
+                for j in HOPS:
                     ref = gram_slots.at[stage, place, span, :]
                     copies.append(send(ref, ref, gram_sem, 2 + 9 * stage + 3 * part + j - 1, along(order[stage], j)))
             yield
@@ -202,7 +214,8 @@
         own, c1s, c1r, s2, sem = bufs["own"], bufs["c1s"], bufs["c1r"], bufs["s2"], bufs["sem"]
         a2r, b2r, s3, r3, shard, g = bufs["a2r"], bufs["b2r"], bufs["s3"], bufs["r3"], bufs["shard"], bufs["gathered"]
         rows = own.shape[2]
-        waves = wave_rows(rows)
+        large = rows > 256
+        waves = wave_rows(rows) if large else (((0, rows // 2), (rows // 2, rows // 2)),)
         zs = [lax.rem(z + 1 + k, SIDE) for k in range(SIDE)]
         span = columns // SIDE
         pieces = 1 if span % 1024 == 0 else 2
@@ -335,7 +348,8 @@
                 for copy in self.cores:
                     copy.wait_recv()
 
-        one, two = Wave(0), Wave(1)
+        parts = [Wave(index) for index in range(len(waves))]
+        one, two = parts[0], parts[-1]
         for k in range(SIDE):
             compute(k)
             if k > 0:
@@ -343,32 +357,33 @@
                 one.second(k - 1)
         add_core(3)
         one.second(3)
-        for k in range(SIDE):
-            two.second(k)
-        one.third()
-        if rows > 256:
+        if large:
+            for k in range(SIDE):
+                two.second(k)
+            one.third()
+        two.third()
+        if large:
             one.finish()
-            two.third()
+            first, count = one.a[0], one.a[1] + one.b[1]
+            gram_own[...] = local_gram(bufs, first, count)
+            two.finish()
+            gram_own[...] += local_gram(bufs, first + count, rows - count)
         else:
-            two.third()
-            one.finish()
-        if gather and rows > 256:
-            one.first_hop()
-        two.finish()
-        steps = gram_steps(bufs)
+            two.finish()
+            gram_own[...] = local_gram(bufs, 0, rows)
+        steps = gram_steps()
         if not gather:
             return steps
         next(steps)
         next(steps)
-        if rows <= 256:
-            one.first_hop()
-        two.first_hop()
+        for wave in parts:
+            wave.first_hop()
         next(steps)
-        one.second_hop()
-        two.second_hop()
+        for wave in parts:
+            wave.second_hop()
         next(steps)
-        one.wait_cores()
-        two.wait_cores()
+        for wave in parts:
+            wave.wait_cores()
         return steps
 
     row_y, row_z = float(SIDE * features), float(SIDE * hidden)
@@ -376,30 +391,33 @@
         sends = []
         if iteration == 0:
             loads[0].wait()
-            for k in range(SIDE):
-                span = pl.ds(pl.multiple_of(turn[k] * tokens, tokens), tokens)
-                loads[1 + k].wait()
-                s_part[span, :] = jnp.zeros((tokens, K), f32)
-
-                @pl.loop(0, SIDE)
+            for k, count in ((0, 2), (2, 1), (3, 1)):
+                for n in range(k, k + count):
+                    loads[1 + n].wait()
+                s_part[quarter(k, count), :] = jnp.zeros((count * tokens, K), f32)
+
+                @pl.loop(0, 2)
                 def _(i):
-                    deep = pl.ds(pl.multiple_of(i * (hidden // SIDE), K), hidden // SIDE)
-                    s_part[span, :] += jnp.dot(o[span, deep], sketch[deep, :], preferred_element_type=f32)
+                    deep = pl.ds(pl.multiple_of(i * (hidden // 2), K), hidden // 2)
+                    s_part[quarter(k, count), :] += jnp.dot(
+                        o[quarter(k, count), deep], sketch[deep, :], preferred_element_type=f32
+                    )
 
                 if k == 0:
                     pl.semaphore_wait(barrier, len(partners))
                 if k < 3:
-                    sends.append(send_tokens(k))
-            loads[5].wait()
+                    sends += [send_tokens(n) for n in range(k, k + count)]
+            for k in range(SIDE):
+                loads[5 + k].wait()
             share_tokens(sends, None)
         else:
             s_part[...] = jnp.zeros(s_part.shape, f32)
-            n = hidden // SIDE
-
-            @pl.loop(0, SIDE)
+            n = hidden // 2
+
+            @pl.loop(0, 2)
             def _(i):
                 deep = pl.ds(pl.multiple_of(i * n, K), n)
-                block = bufs_z["gathered"][i].reshape(n, K)
+                block = bufs_z["gathered"][pl.ds(2 * i, 2)].reshape(n, K)
                 s_part[...] += jnp.dot(o[:, deep], block, preferred_element_type=f32)
 
             sends = [send_tokens(k) for k in range(3)]
@@ -430,6 +448,11 @@
     flush()
 
 
+def copy_out(q_ref, p_ref, q_out, p_out):
+    q_out[...] = q_ref[...]
+    p_out[...] = p_ref[...]
+
+
 def panel_scratch(rows):
     return [
         pltpu.VMEM((4, 4, rows, K), f32),
@@ -456,7 +479,7 @@
         pltpu.VMEM((tokens, features), bf16),
         pltpu.VMEM((tokens, hidden), bf16),
         pltpu.VMEM((hidden, K), bf16),
-        pltpu.SemaphoreType.DMA((6,)),
+        pltpu.SemaphoreType.DMA((9,)),
         pltpu.VMEM((tokens, K), f32),
         pltpu.VMEM((3, quarter, K), f32),
         pltpu.VMEM((quarter, K), bf16),
@@ -488,6 +511,13 @@
         ),
         name="subspace_iteration",
     )(activations, out_grads, sketch)
+    q, p = pl.pallas_call(
+        copy_out,
+        out_shape=(jax.ShapeDtypeStruct(q.shape, f32), jax.ShapeDtypeStruct(p.shape, f32)),
+        in_specs=[pl.BlockSpec(memory_space=pltpu.VMEM)] * 2,
+        out_specs=(pl.BlockSpec(memory_space=pltpu.VMEM), pl.BlockSpec(memory_space=pltpu.VMEM)),
+        name="write_outputs",
+    )(q, p)
     return q.T, p.T
 
 

time: 184 us -> 188 us (1.022); the launches traced: 184 us -> 185 us
  Pallas kernels: 180 us -> 185 us
  local copies, waits for them, and re-layouts: 2.94 us -> 0 us
    unnamed x2 -> x0, local copies, waits for them, and re-layouts: 2.94 us -> none
    pallas_call x1, Pallas kernels: 180 us -> 183 us  [body(): pl.pallas_call(functools.partial(kernel, features, hidden), out_shape=(ja...]
where the time goes in v3:
time: 188 us; the launch traced here: 185 us
  Pallas kernels  185 us (98%)
    pallas_call x1, Pallas kernels, body(): pl.pallas_call(functools.partial(kernel, features, hidden), out_shape=(ja...  183 us

profile of v3, /device:TPU:1, one launch (start us, length us, event | category | flops | bytes accessed | tf_op | source)
XLA Modules:
  0.0 185.4 jit_solution(11923417810254187202)
XLA Ops:
  0.6 182.9 %subspace_iteration.1 = (f32[64,128]{1,0:T(8,128)}, f32[64,416]{1,0:T(8,128)}) custom-call(bf16[512,4096]{1,0:T(8,128)(2,1)} %a_hbm.1, bf16[512,13312]{1,0:T(8,128)(2,1)} %o_hbm.1, bf16[13312,128]{1,0:T(8,128)(2,1)} %sk_hbm.1), custom_call_target="tpu_custom_call" | custom-call | tf_op jit(solution)/shard_map/subspace_iteration/pallas_call | solution.py:500
  183.6 1.6 write_outputs.1

commit v4 on v3

--- a/solution.py
+++ b/solution.py
@@ -124,24 +124,22 @@
         pl.semaphore_signal(barrier, inc=1, device_id=device, device_id_type=pl.DeviceIdType.MESH)
 
     tokens = s_mine.shape[0]
-
-    def quarter(k, count=1):
-        return pl.ds(k * tokens, count * tokens)
-
     turn = [lax.rem(y + hop, SIDE) for hop in (*HOPS, 0)]
     loads = [pltpu.make_async_copy(sk_hbm, sketch, load_sem.at[0])]
-    for held, source, sem in ((o, o_hbm, 1), (a, a_hbm, 5)):
-        for k in range(SIDE):
-            span = pl.ds(pl.multiple_of(turn[k] * tokens, tokens), tokens)
-            loads.append(pltpu.make_async_copy(source.at[span, :], held.at[quarter(k), :], load_sem.at[sem + k]))
+    for k in range(SIDE):
+        span = pl.ds(pl.multiple_of(turn[k] * tokens, tokens), tokens)
+        loads.append(pltpu.make_async_copy(o_hbm.at[span, :], o.at[span, :], load_sem.at[1 + k]))
+    loads.append(pltpu.make_async_copy(a_hbm, a, load_sem.at[5]))
     for copy in loads:
         copy.start()
 
     def send_tokens(k):
-        return send(s_part.at[quarter(k), :], s_recv.at[k], s_sem, k, along("y", HOPS[k]))
+        span = pl.ds(pl.multiple_of(turn[k] * tokens, tokens), tokens)
+        return send(s_part.at[span, :], s_recv.at[k], s_sem, k, along("y", HOPS[k]))
 
     def share_tokens(sends, factor):
-        total = s_part[quarter(3), :]
+        span = pl.ds(pl.multiple_of(y * tokens, tokens), tokens)
+        total = s_part[span, :]
         for k in range(3):
             sends[k].wait_recv()
             total = total + s_recv[k]
@@ -149,19 +147,12 @@
             total = lax.dot_general(
                 total, factor(), (((1,), (1,)), ((), ())), precision=HIGHEST, preferred_element_type=f32
             )
-        s_all[quarter(3), :] = total.astype(bf16)
-        outs = [
-            send(
-                s_all.at[quarter(3), :], s_all.at[quarter(HOPS.index(SIDE - hop)), :], s_sem, 3 + k, along("y", hop)
-            )
-            for k, hop in enumerate(HOPS)
-        ]
-        s_t[:, quarter(3)] = s_all[quarter(3), :].T
-        for copy, hop in zip(outs, HOPS):
+        s_all[span, :] = total.astype(bf16)
+        outs = [send(s_all.at[span, :], s_all.at[span, :], s_sem, 3 + k, along("y", HOPS[k])) for k in range(3)]
+        for copy in outs:
             copy.wait_recv()
-            came = quarter(HOPS.index(SIDE - hop))
-            s_t[:, came] = s_all[came, :].T
         flush()
+        s_t[...] = s_all[...].T
 
     def local_gram(bufs, first, count):
         part = bufs["shard"][first : first + count, :]
@@ -391,33 +382,30 @@
         sends = []
         if iteration == 0:
             loads[0].wait()
-            for k, count in ((0, 2), (2, 1), (3, 1)):
-                for n in range(k, k + count):
-                    loads[1 + n].wait()
-                s_part[quarter(k, count), :] = jnp.zeros((count * tokens, K), f32)
-
-                @pl.loop(0, 2)
+            for k in range(SIDE):
+                span = pl.ds(pl.multiple_of(turn[k] * tokens, tokens), tokens)
+                loads[1 + k].wait()
+                s_part[span, :] = jnp.zeros((tokens, K), f32)
+
+                @pl.loop(0, SIDE)
                 def _(i):
-                    deep = pl.ds(pl.multiple_of(i * (hidden // 2), K), hidden // 2)
-                    s_part[quarter(k, count), :] += jnp.dot(
-                        o[quarter(k, count), deep], sketch[deep, :], preferred_element_type=f32
-                    )
+                    deep = pl.ds(pl.multiple_of(i * (hidden // SIDE), K), hidden // SIDE)
+                    s_part[span, :] += jnp.dot(o[span, deep], sketch[deep, :], preferred_element_type=f32)
 
                 if k == 0:
                     pl.semaphore_wait(barrier, len(partners))
                 if k < 3:
-                    sends += [send_tokens(n) for n in range(k, k + count)]
-            for k in range(SIDE):
-                loads[5 + k].wait()
+                    sends.append(send_tokens(k))
+            loads[5].wait()
             share_tokens(sends, None)
         else:
             s_part[...] = jnp.zeros(s_part.shape, f32)
-            n = hidden // 2
-
-            @pl.loop(0, 2)
+            n = hidden // SIDE
+
+            @pl.loop(0, SIDE)
             def _(i):
                 deep = pl.ds(pl.multiple_of(i * n, K), n)
-                block = bufs_z["gathered"][pl.ds(2 * i, 2)].reshape(n, K)
+                block = bufs_z["gathered"][i].reshape(n, K)
                 s_part[...] += jnp.dot(o[:, deep], block, preferred_element_type=f32)
 
             sends = [send_tokens(k) for k in range(3)]
@@ -479,7 +467,7 @@
         pltpu.VMEM((tokens, features), bf16),
         pltpu.VMEM((tokens, hidden), bf16),
         pltpu.VMEM((hidden, K), bf16),
-        pltpu.SemaphoreType.DMA((9,)),
+        pltpu.SemaphoreType.DMA((6,)),
         pltpu.VMEM((tokens, K), f32),
         pltpu.VMEM((3, quarter, K), f32),
         pltpu.VMEM((quarter, K), bf16),

time: 188 us -> 179 us (0.952); the launches traced: 185 us -> 179 us
  Pallas kernels: 185 us -> 178 us
    pallas_call x1, Pallas kernels: 183 us -> 176 us  [body(): pl.pallas_call(functools.partial(kernel, features, hidden), out_shape=(ja...]
where the time goes in v4:
time: 179 us
  Pallas kernels  178 us (99%)
    pallas_call x1, Pallas kernels, body(): pl.pallas_call(functools.partial(kernel, features, hidden), out_shape=(ja...  176 us

profile of v4, /device:TPU:1, one launch (start us, length us, event | category | flops | bytes accessed | tf_op | source)
XLA Modules:
  0.0 178.7 jit_solution(1865145851262405166)
XLA Ops:
  0.6 176.4 %subspace_iteration.1 = (f32[64,128]{1,0:T(8,128)}, f32[64,416]{1,0:T(8,128)}) custom-call(bf16[512,4096]{1,0:T(8,128)(2,1)} %a_hbm.1, bf16[512,13312]{1,0:T(8,128)(2,1)} %o_hbm.1, bf16[13312,128]{1,0:T(8,128)(2,1)} %sk_hbm.1), custom_call_target="tpu_custom_call" | custom-call | tf_op jit(solution)/shard_map/subspace_iteration/pallas_call | solution.py:488
  177.1 1.6 write_outputs.1
